TPU v7x, 32 devices: a whole 2x2x4 slice. The times are simulated.
32 devices in a mesh: dp: 16 (over z, y, core), seq: 2 (over x).
Axes of the slice: x: 2, y: 2, z: 4, core: 2. Of those that a mesh axis runs over, the one named last changes fastest.
Arguments:
- tile_feats: bfloat16 [8192, 2048], P('dp'), may hold values from -6 to 6
- tile_pos: int32 [16, 512], P('dp'), may hold values from -1 to 511, as said below
- slide_count: int32 [16], P('dp'), may hold values from 128 to 512, as said below
- w_proj: bfloat16 [2048, 768], P(None, 'seq'), may hold values from -0.125 to 0.125
- emb_grad: bfloat16 [16, 512, 768], P('dp', 'seq'), may hold values from -6 to 6
- ln_gain: float32 [768], replicated, may hold values from 0.25 to 1.75
- w_qkv: bfloat16 [768, 2304], P('dp'), may hold values from -1.5 to 1.5
- w_out: bfloat16 [768, 768], P('dp'), may hold values from -0.21875 to 0.21875
Outputs:
- slide_emb: bfloat16 [16, 512, 768], P('dp', 'seq')
- attn_branch: bfloat16 [16, 512, 768], P('dp', 'seq')
- proj_grad: float32 [2048, 768], P(None, 'seq')
Inputs may be any that keep to these rules, and one draw needn't show every extreme that they name: `tile_pos`: slot j of a row belongs to slide j // 32. Each position below a slide's slide_count is held by exactly one slot of that slide over all rows; all other slots hold -1. `slide_count`: some slide is full.
All inputs are finite; a program needn't handle non-finite values.
Results may differ from a plain program's by a relative error of at most 0.017.
The roundings to bfloat16 on the way count: a program that leaves them out, or rounds other values in their place, can miss the bound.
Values may be sent and summed in bfloat16 or wider, within the bound.
A program may use at most 128 MiB of HBM per device.

v0:
```python
import jax
import jax.numpy as jnp
from jax import lax
from jax.sharding import PartitionSpec as P

D = 768
HEAD_COUNT = 12
HEAD_WIDTH = 64
DILATION_STEP = 4
NEGATIVE = -1e30
EPSILON = 1e-05


def selection_shift(values, heads, dilation):
    length = values.shape[1]
    rest = values.shape[2:]
    shaped = values.reshape((heads, length // dilation, dilation) + rest)
    return jnp.stack(
        [shaped[head_number, :, head_number % dilation] for head_number in range(heads)]
    )


def insertion_shift(values, chosen, heads, dilation):
    length = values.shape[1]
    rest = values.shape[2:]
    shaped = values.reshape((heads, length // dilation, dilation) + rest)
    shift_amounts = jnp.arange(heads, dtype=jnp.int32) % dilation
    select = jnp.arange(dilation, dtype=jnp.int32)[None, :] == shift_amounts[:, None]
    select = select.reshape((heads, 1, dilation) + (1,) * len(rest))
    merged = jnp.where(select, chosen[:, :, None], shaped)
    return merged.reshape(values.shape)


def local(tile_feats, tile_pos, slide_count, w_proj, emb_grad, ln_gain, w_qkv, w_out):
    seq_count = lax.axis_size("seq")
    seq_index = lax.axis_index("seq")
    slot_rows = tile_feats.shape[0]
    nearby_length = emb_grad.shape[1]
    slide_len = nearby_length * seq_count
    inner = HEAD_COUNT * HEAD_WIDTH
    scale = HEAD_WIDTH ** (-0.5)
    tile_count = slide_count[0]
    emb_part = jnp.dot(tile_feats, w_proj, preferred_element_type=jnp.float32).astype(jnp.bfloat16)
    feature_part = emb_part.shape[1]
    positions = tile_pos.reshape(slot_rows)
    arrived, arrived_pos = (
        lax.all_to_all(emb_part, "dp", split_axis=0, concat_axis=0, tiled=True),
        lax.all_to_all(positions, "dp", split_axis=0, concat_axis=0, tiled=True),
    )
    target = jnp.where(arrived_pos >= 0, arrived_pos, slide_len).astype(jnp.int32)
    slide_rows = (
        jnp.zeros((slide_len + 1, feature_part), jnp.bfloat16).at[target].set(arrived)[:slide_len]
    )
    local_emb = lax.all_to_all(slide_rows, "seq", split_axis=0, concat_axis=1, tiled=True)
    widened = local_emb.astype(jnp.float32)
    center = jnp.mean(widened, axis=-1, keepdims=True)
    spread = jnp.mean(jnp.square(widened - center), axis=-1, keepdims=True)
    normed = ((widened - center) * lax.rsqrt(spread + EPSILON) * ln_gain).astype(jnp.bfloat16)
    columns = normed
    projected = jnp.dot(
        columns, lax.all_gather(w_qkv, "dp", axis=0, tiled=True), preferred_element_type=jnp.float32
    )
    projected = projected.astype(jnp.bfloat16)
    query_rows = projected[:, :inner].reshape(nearby_length, HEAD_COUNT, HEAD_WIDTH)
    key_matrix = projected[:, inner : 2 * inner].reshape(nearby_length, HEAD_COUNT, HEAD_WIDTH)
    value_matrix = projected[:, 2 * inner :].reshape(nearby_length, HEAD_COUNT, HEAD_WIDTH)
    sequence_position = seq_index * nearby_length + jnp.arange(nearby_length, dtype=jnp.int32)
    occupied = sequence_position < tile_count
    shift_amounts = jnp.arange(HEAD_COUNT, dtype=jnp.int32) % DILATION_STEP
    local_scores = (
        jnp.einsum("qhd,khd->hqk", query_rows, key_matrix, preferred_element_type=jnp.float32)
        * scale
    )
    local_ok = jnp.broadcast_to(occupied[None, None, :], local_scores.shape)
    nearby_maximum = jnp.max(jnp.where(local_ok, local_scores, NEGATIVE), axis=-1)
    local_weight = jnp.where(local_ok, jnp.exp(local_scores - nearby_maximum[..., None]), 0.0)
    nearby_sum = jnp.sum(local_weight, axis=-1)
    nearby_accumulator = jnp.einsum("hqk,khd->hqd", local_weight, value_matrix.astype(jnp.float32))
    stepped_queries = query_rows.reshape(
        nearby_length // DILATION_STEP, DILATION_STEP, HEAD_COUNT, HEAD_WIDTH
    )
    selected_query = jnp.stack(
        [
            stepped_queries[:, head_number % DILATION_STEP, head_number, :]
            for head_number in range(HEAD_COUNT)
        ]
    )
    key_value = jnp.concatenate([key_matrix, value_matrix], axis=-1)
    flat_rows = key_value.reshape(nearby_length, HEAD_COUNT * 2 * HEAD_WIDTH)
    portion = lax.all_gather(flat_rows, "seq", axis=0, tiled=True)
    row_counts = portion.shape[0]
    head_split = (row_counts + DILATION_STEP - 1) // DILATION_STEP
    shaped = portion.reshape(row_counts, HEAD_COUNT, 2 * HEAD_WIDTH)
    leading_index = shift_amounts % DILATION_STEP
    index_of_row = (
        leading_index[:, None] + DILATION_STEP * jnp.arange(head_split, dtype=jnp.int32)[None, :]
    )
    inside = index_of_row < row_counts
    safe_index = jnp.minimum(index_of_row, row_counts - 1)
    head_index = jnp.arange(HEAD_COUNT, dtype=jnp.int32)[:, None]
    chosen = shaped[safe_index, head_index, :]
    key_ok = inside & (index_of_row < tile_count)
    previous_maximum = selection_shift(nearby_maximum, HEAD_COUNT, DILATION_STEP)
    previous_sum = selection_shift(nearby_sum, HEAD_COUNT, DILATION_STEP)
    previous_accumulator = selection_shift(nearby_accumulator, HEAD_COUNT, DILATION_STEP)
    far_scores = (
        jnp.einsum(
            "hqd,hkd->hqk",
            selected_query,
            chosen[..., :HEAD_WIDTH],
            preferred_element_type=jnp.float32,
        )
        * scale
    )
    usable = jnp.broadcast_to(key_ok[:, None, :], far_scores.shape)
    new_max = jnp.maximum(
        previous_maximum, jnp.max(jnp.where(usable, far_scores, NEGATIVE), axis=-1)
    )
    far_weight = jnp.where(usable, jnp.exp(far_scores - new_max[..., None]), 0.0)
    rescale = jnp.exp(previous_maximum - new_max)
    updated_sum = previous_sum * rescale + jnp.sum(far_weight, axis=-1)
    updated_accumulator = previous_accumulator * rescale[..., None] + jnp.einsum(
        "hqk,hkd->hqd", far_weight, chosen[..., HEAD_WIDTH:].astype(jnp.float32)
    )
    complete_sum = insertion_shift(nearby_sum, updated_sum, HEAD_COUNT, DILATION_STEP)
    complete_accumulator = insertion_shift(
        nearby_accumulator, updated_accumulator, HEAD_COUNT, DILATION_STEP
    )
    safe_total = jnp.where(occupied[None, :], complete_sum, 1.0)
    context = jnp.where(occupied[None, :, None], complete_accumulator / safe_total[..., None], 0.0)
    context = context.transpose(1, 0, 2).reshape(nearby_length, inner).astype(jnp.bfloat16)
    columns = context
    branch_out = jnp.dot(
        columns, lax.all_gather(w_out, "dp", axis=0, tiled=True), preferred_element_type=jnp.float32
    )
    attn_branch = branch_out.astype(jnp.bfloat16)
    returned_grad = lax.all_to_all(
        emb_grad.reshape(nearby_length, D), "seq", split_axis=1, concat_axis=0, tiled=True
    )
    padded_grad = jnp.concatenate(
        [returned_grad, jnp.zeros((1, feature_part), jnp.bfloat16)], axis=0
    )
    picked_grad = padded_grad[target]
    slot_grad = lax.all_to_all(picked_grad, "dp", split_axis=0, concat_axis=0, tiled=True)
    grad_part = lax.dot_general(
        tile_feats, slot_grad, (((0,), (0,)), ((), ())), preferred_element_type=jnp.float32
    )
    proj_grad = lax.psum(grad_part, "dp")
    return (local_emb[None], attn_branch[None], proj_grad)


def solution(mesh):
    in_specs = (
        P("dp", None),
        P("dp", None),
        P("dp"),
        P(None, "seq"),
        P("dp", "seq", None),
        P(),
        P("dp", None),
        P("dp", None),
    )
    out_specs = (P("dp", "seq", None), P("dp", "seq", None), P(None, "seq"))
    return jax.shard_map(local, mesh=mesh, in_specs=in_specs, out_specs=out_specs, check_vma=False)
```

profile of v0, /device:TPU:0, one launch (start us, length us, event | category | flops | bytes accessed | tf_op | source)
XLA Modules:
  0.0 267.3 jit_solution(15064173347911541342)
XLA Ops:
  7.2 0.7 all-gather.4.cloned.1.call-update
  8.4 1.3 reduce.56
  9.8 0.7 all_to_all.50
  10.5 7.4 %all-to-all-start = ((s32[16,32,1]{1,2,0:T(1,128)}), s32[16,32,1]{1,2,0:T(1,128)S(1)}, u32[]{:S(2)}, u32[]{:S(2)}) async-start(s32[16,32,1]{1,2,0:T(1,128)} %all_to_all.50), calls=%async_computation | async-start | bytes 16384 | tf_op jit(solution)/shard_map/all_to_all | solution.py:48
  17.9 3.5 %convolution_convert_fusion.2 = bf16[512,384]{1,0:T(8,128)(2,1)} fusion(bf16[512,2048]{1,0:T(8,128)(2,1)S(1)} %copy-done, bf16[2048,384]{1,0:T(8,128)(2,1)} %param.11), kind=kOutput, calls=%fused_computation.14 | convolution fusion | flops 805502976 | bytes 4063232 | tf_op jit(solution)/shard_map/dot_general | solution.py:43
  21.3 2.9 %all-to-all-done = s32[16,32,1]{1,2,0:T(1,128)S(1)} async-done(((s32[16,32,1]{1,2,0:T(1,128)}), s32[16,32,1]{1,2,0:T(1,128)S(1)}, u32[]{:S(2)}, u32[]{:S(2)}) %all-to-all-start) | async-done | bytes 2080 | tf_op jit(solution)/shard_map/all_to_all | solution.py:48
  24.2 3.6 %all-to-all-start.1 = ((bf16[16,32,384]{2,1,0:T(8,128)(2,1)}), bf16[16,32,384]{2,1,0:T(8,128)(2,1)S(1)}, u32[]{:S(2)}, u32[]{:S(2)}) async-start(bf16[16,32,384]{2,1,0:T(8,128)(2,1)} %bitcast.1), calls=%async_computation.1 | async-start | bytes 786432 | tf_op jit(solution)/shard_map/all_to_all | solution.py:47
  27.9 0.8 copy.164
  28.6 0.7 reduce.57
  29.4 12.1 %all-to-all-done.1 = bf16[16,32,384]{2,1,0:T(8,128)(2,1)S(1)} async-done(((bf16[16,32,384]{2,1,0:T(8,128)(2,1)}), bf16[16,32,384]{2,1,0:T(8,128)(2,1)S(1)}, u32[]{:S(2)}, u32[]{:S(2)}) %all-to-all-start.1) | async-done | bytes 393248 | tf_op jit(solution)/shard_map/all_to_all | solution.py:47
  41.5 0.7 copy-done.3
  42.2 3.5 %all-to-all-start.3 = ((bf16[256,2,384]{2,0,1:T(8,128)(2,1)}), bf16[256,2,384]{2,0,1:T(8,128)(2,1)S(1)}, u32[]{:S(2)}, u32[]{:S(2)}) async-start(bf16[256,2,384]{2,0,1:T(8,128)(2,1)} %copy.164), calls=%async_computation.3 | async-start | bytes 786432 | tf_op jit(solution)/shard_map/all_to_all | solution.py:137
  45.7 2.9 %scatter_custom_fusion = bf16[513,384]{1,0:T(8,128)(2,1)S(1)} fusion(s32[512]{0:T(512)S(1)} %bitcast.199, bf16[512,384]{1,0:T(8,128)(2,1)} %bitcast.185, bf16[]{:T(256)} %constant.24.clone.1), kind=kCustom, calls=%fused_computation.31 | custom fusion | bytes 394496 | tf_op jit(solution)/shard_map/scatter | solution.py:52
  48.6 0.8 slice.220
  49.4 3.2 %all-to-all-done.3 = bf16[256,2,384]{2,0,1:T(8,128)(2,1)S(1)} async-done(((bf16[256,2,384]{2,0,1:T(8,128)(2,1)}), bf16[256,2,384]{2,0,1:T(8,128)(2,1)S(1)}, u32[]{:S(2)}, u32[]{:S(2)}) %all-to-all-start.3) | async-done | bytes 393248 | tf_op jit(solution)/shard_map/all_to_all | solution.py:137
  52.6 3.5 %all-to-all-start.2 = ((bf16[2,256,384]{2,1,0:T(8,128)(2,1)}), bf16[2,256,384]{2,1,0:T(8,128)(2,1)S(1)}, u32[]{:S(2)}, u32[]{:S(2)}) async-start(bf16[2,256,384]{2,1,0:T(8,128)(2,1)} %bitcast.3), calls=%async_computation.2 | async-start | bytes 786432 | tf_op jit(solution)/shard_map/all_to_all | solution.py:54
  56.1 2.6 gather_fusion.1
  58.7 3.5 %all-to-all-done.2 = bf16[2,256,384]{2,1,0:T(8,128)(2,1)S(1)} async-done(((bf16[2,256,384]{2,1,0:T(8,128)(2,1)}), bf16[2,256,384]{2,1,0:T(8,128)(2,1)S(1)}, u32[]{:S(2)}, u32[]{:S(2)}) %all-to-all-start.2) | async-done | bytes 393248 | tf_op jit(solution)/shard_map/all_to_all | solution.py:54
  62.1 4.8 %all-to-all-start.4 = ((bf16[16,32,384]{2,1,0:T(8,128)(2,1)}), bf16[16,32,384]{2,1,0:T(8,128)(2,1)}, u32[]{:S(2)}, u32[]{:S(2)}) async-start(bf16[16,32,384]{2,1,0:T(8,128)(2,1)} %bitcast.50), calls=%async_computation.4 | async-start | bytes 786432 | tf_op jit(solution)/shard_map/all_to_all | solution.py:144
  67.0 0.9 bitcast_convert_fusion
  67.9 1.4 copy.125
  69.3 9.9 %all-to-all-done.4 = bf16[16,32,384]{2,1,0:T(8,128)(2,1)} async-done(((bf16[16,32,384]{2,1,0:T(8,128)(2,1)}), bf16[16,32,384]{2,1,0:T(8,128)(2,1)}, u32[]{:S(2)}, u32[]{:S(2)}) %all-to-all-start.4) | async-done | bytes 393248 | tf_op jit(solution)/shard_map/all_to_all | solution.py:144
  79.2 3.7 %convolution_bitcast_fusion = f32[2048,384]{0,1:T(8,128)} fusion(bf16[512,384]{1,0:T(8,128)(2,1)} %bitcast.51, bf16[512,2048]{1,0:T(8,128)(2,1)S(1)} %copy-done), kind=kOutput, calls=%fused_computation.6 | convolution fusion | flops 805306368 | bytes 5636096 | tf_op jit(solution)/shard_map/dot_general | solution.py:145
  83.5 0.9 fusion.9
  84.4 3.5 %convolution_convert_fusion = bf16[256,2304]{1,0:T(8,128)(2,1)S(1)} fusion(bf16[256,768]{0,1:T(8,128)(2,1)} %fusion.9, bf16[768,2304]{1,0:T(8,128)(2,1)} %all-gather.4.cloned.1.call-done), kind=kOutput, calls=%fused_computation.3 | convolution fusion | flops 906559488 | bytes 5111808 | tf_op jit(solution)/shard_map/dot_general | solution.py:60
  87.9 0.8 fusion.28
  88.8 0.9 copy.128
  89.7 1.2 copy.127
  90.8 2.0 pad_maximum_fusion
  94.4 0.9 copy.123
  95.3 1.9 copy.165
  97.2 87.1 %all-reduce.3.cloned.1.call-done = f32[2048,384]{0,1:T(8,128)} async-done(((f32[2048,384]{0,1:T(8,128)}), f32[2048,384]{0,1:T(8,128)}) %all-reduce.3.cloned.1.call-update) | async-done | bytes 3145744 | tf_op jit(solution)/shard_map/psum | solution.py:148
  184.4 3.5 %copy.166 = f32[2048,384]{1,0:T(8,128)} copy(f32[2048,384]{0,1:T(8,128)} %all-reduce.3.cloned.1.call-done) | data formatting | bytes 6291456
  188.1 1.6 reshape_reshape.3
  189.7 2.4 select_reduce_fusion
  192.1 2.8 %fusion.1 = f32[12,256,64]{1,2,0:T(8,128)S(1)} fusion(bf16[256,12,64]{0,2,1:T(8,128)(2,1)} %bitcast.181, f32[12,256,256]{1,2,0:T(8,128)} %get-tuple-element.69, f32[12,256]{1,0:T(8,128)S(1)} %get-tuple-element.68, pred[256]{0:T(512)(128)(4,1)S(1)} %add_compare_fusion.2), kind=kOutput, calls=%fused_computation.8 | convolution fusion | flops 103022592 | bytes 4337920 | tf_op jit(solution)/shard_map/hqk,khd->hqd/dot_general | solution.py:78
  195.3 0.7 fusion
  195.9 1.7 copy.130
  197.6 2.5 fusion.27
  200.7 2.6 fusion.29
  203.3 3.4 %slice_reduce_fusion.12 = (f32[64]{0:T(128)S(1)}, f32[64]{0:T(128)S(1)}, f32[64]{0:T(128)S(1)}, f32[64]{0:T(128)}, f32[64]{0:T(128)}, /*index=5*/f32[64]{0:T(128...) fusion(f32[12,64,4]{0,2,1:T(4,128)S(1)} %bitcast.175), kind=kLoop, calls=%fused_computation.72 | loop fusion | bytes 6144 | tf_op jit(solution)/shard_map/slice | solution.py:19
  206.8 3.4 %slice_reduce_fusion = (f32[64]{0:T(128)}, f32[64]{0:T(128)}, f32[64]{0:T(128)}, f32[64]{0:T(128)}, f32[64]{0:T(128)}, /*index=5*/f32[64]{0:T(128)}, f32[64]{0:T...) fusion(f32[12,64,4]{0,2,1:T(4,128)S(1)} %bitcast.176), kind=kLoop, calls=%fused_computation.60 | loop fusion | bytes 6144 | tf_op jit(solution)/shard_map/slice | solution.py:19
  210.1 1.4 constant_dynamic-update-slice_fusion.10
  211.5 1.4 constant_dynamic-update-slice_fusion.9
  212.9 1.4 constant_dynamic-update-slice_fusion.8
  214.3 1.4 constant_dynamic-update-slice_fusion.7
  215.6 1.4 constant_dynamic-update-slice_fusion.6
  217.0 1.4 constant_dynamic-update-slice_fusion.5
  218.4 1.4 constant_dynamic-update-slice_fusion.4
  219.8 1.4 constant_dynamic-update-slice_fusion.3
  221.1 1.4 constant_dynamic-update-slice_fusion.2
  222.5 0.8 constant_dynamic-update-slice_fusion.22
  223.3 0.8 constant_dynamic-update-slice_fusion.21
  224.0 0.8 constant_dynamic-update-slice_fusion.20
  224.8 0.8 constant_dynamic-update-slice_fusion.19
  226.2 1.3 stack.73
  227.6 1.4 stack.87
  229.7 2.6 copy.156
  232.3 17.9 %gather_fusion = bf16[1536,128]{1,0:T(8,128)(2,1)S(1)} fusion(bf16[512,12,128]{2,0,1:T(8,128)(2,1)} %copy.156, s32[1536]{0:T(1024)S(1)} %fusion.21), kind=kCustom, calls=%fused_computation | custom fusion | bytes 798720 | tf_op jit(solution)/shard_map/gather | solution.py:101
  251.0 1.4 convolution_add_fusion
  252.5 1.5 broadcast_in_dim.146
  253.9 2.8 %copy.159 = f32[12,256,64]{1,2,0:T(8,128)} copy(f32[12,256,64]{2,1,0:T(8,128)} %bitcast.168) | data formatting | bytes 1572864 | tf_op jit(solution)/shard_map/jit(_where)/broadcast_in_dim | solution.py:30
  256.9 1.4 select_convert_fusion
  258.3 2.5 fusion.6
  (60 shorter events, 6.0 us)
Async XLA Ops:
  7.2 10.7 %copy-start = (bf16[512,2048]{1,0:T(8,128)(2,1)S(1)}, bf16[512,2048]{1,0:T(8,128)(2,1)}, u32[]{:S(2)}) copy-start(bf16[512,2048]{1,0:T(8,128)(2,1)} %param.8) | copy-start | bytes 6291460
  7.2 77.3 %all-gather.4.cloned.1.call-start = ((), (), s32[]{:S(2)}) async-start(), calls=%async_computation.5 | async-start | bytes 3760128 | tf_op jit(solution)/shard_map/all_gather | solution.py:61
  10.5 13.7 %all-to-all-start = ((s32[16,32,1]{1,2,0:T(1,128)}), s32[16,32,1]{1,2,0:T(1,128)S(1)}, u32[]{:S(2)}, u32[]{:S(2)}) async-start(s32[16,32,1]{1,2,0:T(1,128)} %all_to_all.50), calls=%async_computation | async-start | bytes 16384 | tf_op jit(solution)/shard_map/all_to_all | solution.py:48
  17.9 9.9 %copy-start.2 = (bf16[1,256,768]{2,1,0:T(8,128)(2,1)S(1)}, bf16[1,256,768]{2,1,0:T(8,128)(2,1)}, u32[]{:S(2)}) copy-start(bf16[1,256,768]{2,1,0:T(8,128)(2,1)} %param.12) | copy-start | bytes 1179652
  24.2 17.3 %all-to-all-start.1 = ((bf16[16,32,384]{2,1,0:T(8,128)(2,1)}), bf16[16,32,384]{2,1,0:T(8,128)(2,1)S(1)}, u32[]{:S(2)}, u32[]{:S(2)}) async-start(bf16[16,32,384]{2,1,0:T(8,128)(2,1)} %bitcast.1), calls=%async_computation.1 | async-start | bytes 786432 | tf_op jit(solution)/shard_map/all_to_all | solution.py:47
  41.5 0.7 copy-start.3
  42.2 10.3 %all-to-all-start.3 = ((bf16[256,2,384]{2,0,1:T(8,128)(2,1)}), bf16[256,2,384]{2,0,1:T(8,128)(2,1)S(1)}, u32[]{:S(2)}, u32[]{:S(2)}) async-start(bf16[256,2,384]{2,0,1:T(8,128)(2,1)} %copy.164), calls=%async_computation.3 | async-start | bytes 786432 | tf_op jit(solution)/shard_map/all_to_all | solution.py:137
  52.6 9.6 %all-to-all-start.2 = ((bf16[2,256,384]{2,1,0:T(8,128)(2,1)}), bf16[2,256,384]{2,1,0:T(8,128)(2,1)S(1)}, u32[]{:S(2)}, u32[]{:S(2)}) async-start(bf16[2,256,384]{2,1,0:T(8,128)(2,1)} %bitcast.3), calls=%async_computation.2 | async-start | bytes 786432 | tf_op jit(solution)/shard_map/all_to_all | solution.py:54
  62.1 17.0 %all-to-all-start.4 = ((bf16[16,32,384]{2,1,0:T(8,128)(2,1)}), bf16[16,32,384]{2,1,0:T(8,128)(2,1)}, u32[]{:S(2)}, u32[]{:S(2)}) async-start(bf16[16,32,384]{2,1,0:T(8,128)(2,1)} %bitcast.50), calls=%async_computation.4 | async-start | bytes 786432 | tf_op jit(solution)/shard_map/all_to_all | solution.py:144
  66.9 117.5 %all-reduce.3.cloned.1.call-start = ((), (), s32[]{:S(2)}) async-start(), calls=%async_computation.8 | async-start | bytes 6291456 | tf_op jit(solution)/shard_map/psum | solution.py:148
  82.8 0.7 copy-start.4
  82.9 146.8 %all-gather.6.cloned.1.call-start = ((), (), s32[]{:S(2)}) async-start(), calls=%async_computation.6 | async-start | bytes 2359296 | tf_op jit(solution)/shard_map/all_gather | solution.py:90
  92.8 165.5 %all-gather.8.cloned.1.call-start = ((), (), s32[]{:S(2)}) async-start(), calls=%async_computation.7 | async-start | bytes 1253376 | tf_op jit(solution)/shard_map/all_gather | solution.py:134
  192.1 3.1 %copy-start.1 = (f32[12,256,256]{1,2,0:T(8,128)S(1)}, f32[12,256,256]{1,2,0:T(8,128)}, u32[]{:S(2)}) copy-start(f32[12,256,256]{1,2,0:T(8,128)} %get-tuple-element.69) | copy-start | bytes 9437188
Sparse Core Ops, SparseCore 0:
  10.3 52.3 all-gather.3
  83.0 101.3 all-reduce.2
  185.9 26.3 all-gather.5
  214.4 38.3 all-gather.7
where the time goes:
time: 269 us; the launch traced here: 267 us
  waiting for transfers between devices  120 us (45%)
  local copies, waits for them, and re-layouts  81 us (30%)
  starting transfers between devices  23 us (9%)
  matrix products  20.2 us (8%)
  between operations  14.7 us (5%)
  other arithmetic  8.78 us (3%)
    psum x1, waiting for transfers between devices, local(): proj_grad = lax.psum(grad_part, 'dp')  87.1 us
    unnamed x35, local copies, waits for them, and re-layouts  24 us
    gather x1, local copies, waits for them, and re-layouts, local(): chosen = shaped[safe_index, head_index, :]  17.9 us
    all_to_all x1, waiting for transfers between devices, local(): lax.all_to_all(emb_part, 'dp', split_axis=0, concat_axis=0, tiled=True)  12.1 us
    all_to_all x1, waiting for transfers between devices, local(): lax.all_to_all(picked_grad, 'dp', split_axis=0, concat_axis=0, tiled=True)  9.87 us
    slice x3, local copies, waits for them, and re-layouts, selection_shift(): shaped[head_number, :, head_number % dilation]  9.23 us
    all_to_all x1, starting transfers between devices, local(): lax.all_to_all(positions, 'dp', split_axis=0, concat_axis=0, tiled=True)  7.39 us
  transfers between devices with their start and end apart: 9, of which 6 were waited for; matrix products, arithmetic and copies ran while one was open for 39% of the time, Pallas kernels for 0%

commit v1 on v0

--- a/solution.py
+++ b/solution.py
@@ -9,6 +9,15 @@
 DILATION_STEP = 4
 NEGATIVE = -1e30
 EPSILON = 1e-05
+
+
+def added_up(x, name):
+    size = lax.axis_size(name)
+    total, far = (x, 1)
+    while far < size:
+        total = total + lax.ppermute(total, name, [(i, i ^ far) for i in range(size)])
+        far = 2 * far
+    return total
 
 
 def selection_shift(values, heads, dilation):
@@ -145,7 +154,7 @@
     grad_part = lax.dot_general(
         tile_feats, slot_grad, (((0,), (0,)), ((), ())), preferred_element_type=jnp.float32
     )
-    proj_grad = lax.psum(grad_part, "dp")
+    proj_grad = added_up(grad_part, "dp")
     return (local_emb[None], attn_branch[None], proj_grad)
 
 

time: 269 us -> 405 us (1.51)
  waiting for transfers between devices: 120 us -> 251 us
  local copies, waits for them, and re-layouts: 81 us -> 58.8 us
  other arithmetic: 8.78 us -> 25.7 us
  blocking collectives: 0 us -> 9.53 us
    ppermute x0 -> x4, waiting for transfers between devices: none -> 216 us  [added_up(): lax.ppermute(total, name, [(i, i ^ far) for i in range(size)])]
    psum x1 -> x0, waiting for transfers between devices: 87.1 us -> none  [local(): proj_grad = lax.psum(grad_part, 'dp')]
    add x0 -> x4, other arithmetic: none -> 18 us  [added_up(): total + lax.ppermute(total, name, [(i, i ^ far) for i in range(size)])]
    gather x1, local copies, waits for them, and re-layouts: 17.9 us -> 8.07 us  [local(): chosen = shaped[safe_index, head_index, :]]
    all_to_all x0 -> x1, blocking collectives: none -> 9.53 us  [local(): lax.all_to_all(slide_rows, 'seq', split_axis=0, concat_axis=1, tiled=True)]
    all_to_all x1, waiting for transfers between devices: 9.87 us -> 15.3 us  [local(): lax.all_to_all(picked_grad, 'dp', split_axis=0, concat_axis=0, tiled=True)]
    unnamed x35 -> x45, local copies, waits for them, and re-layouts: 24 us -> 20.1 us
  transfers between devices with their start and end apart: 9 -> 11, of which waited for: 6 -> 7; matrix products, arithmetic and copies ran while one was open for 39% -> 23% of each run, Pallas kernels for 0% -> 0%
where the time goes in v1:
time: 405 us; the launch traced here: 404 us
  waiting for transfers between devices  251 us (62%)
  local copies, waits for them, and re-layouts  58.8 us (15%)
  other arithmetic  25.7 us (6%)
  starting transfers between devices  25.4 us (6%)
  matrix products  18.1 us (4%)
  between operations  14.9 us (4%)
  blocking collectives  9.53 us (2%)
    ppermute x4, waiting for transfers between devices, added_up(): lax.ppermute(total, name, [(i, i ^ far) for i in range(size)])  216 us
    unnamed x45, local copies, waits for them, and re-layouts  20.1 us
    add x4, other arithmetic, added_up(): total + lax.ppermute(total, name, [(i, i ^ far) for i in range(size)])  18 us
    all_to_all x1, waiting for transfers between devices, local(): lax.all_to_all(picked_grad, 'dp', split_axis=0, concat_axis=0, tiled=True)  15.3 us
    all_to_all x1, blocking collectives, local(): lax.all_to_all(slide_rows, 'seq', split_axis=0, concat_axis=1, tiled=True)  9.53 us
    all_to_all x1, waiting for transfers between devices, local(): lax.all_to_all(emb_part, 'dp', split_axis=0, concat_axis=0, tiled=True)  9.07 us
    slice x3, local copies, waits for them, and re-layouts, selection_shift(): shaped[head_number, :, head_number % dilation]  8.7 us
  transfers between devices with their start and end apart: 11, of which 7 were waited for; matrix products, arithmetic and copies ran while one was open for 23% of the time, Pallas kernels for 0%

profile of v1, /device:TPU:0, one launch (start us, length us, event | category | flops | bytes accessed | tf_op | source)
XLA Modules:
  0.0 403.7 jit_solution(5550719582075508399)
XLA Ops:
  7.2 0.7 all-gather.4.cloned.1.call-update
  8.4 1.3 reduce.56
  9.8 0.7 all_to_all.50
  10.5 7.4 %all-to-all-start = ((s32[16,32,1]{1,2,0:T(1,128)}), s32[16,32,1]{1,2,0:T(1,128)S(1)}, u32[]{:S(2)}, u32[]{:S(2)}) async-start(s32[16,32,1]{1,2,0:T(1,128)} %all_to_all.50), calls=%async_computation | async-start | bytes 16384 | tf_op jit(solution)/shard_map/all_to_all | solution.py:57
  17.9 1.1 all_to_all.59
  18.9 0.8 copy.164
  19.7 4.4 %all-to-all-done = s32[16,32,1]{1,2,0:T(1,128)S(1)} async-done(((s32[16,32,1]{1,2,0:T(1,128)}), s32[16,32,1]{1,2,0:T(1,128)S(1)}, u32[]{:S(2)}, u32[]{:S(2)}) %all-to-all-start) | async-done | bytes 2080 | tf_op jit(solution)/shard_map/all_to_all | solution.py:57
  24.2 3.5 all-to-all-start.3
  27.7 0.7 reduce.57
  28.4 6.0 %all-to-all-done.3 = bf16[256,2,384]{2,0,1:T(8,128)(2,1)S(1)} async-done(((bf16[256,2,384]{2,0,1:T(8,128)(2,1)}), bf16[256,2,384]{2,0,1:T(8,128)(2,1)S(1)}, u32[]{:S(2)}, u32[]{:S(2)}) %all-to-all-start.3) | async-done | bytes 393248 | tf_op jit(solution)/shard_map/all_to_all | solution.py:146
  34.5 2.6 gather_fusion.1
  37.1 3.6 all-to-all-start.4
  40.7 3.4 convolution_convert_fusion.2
  44.1 15.3 %all-to-all-done.4 = bf16[16,32,384]{2,1,0:T(8,128)(2,1)S(1)} async-done(((bf16[16,32,384]{2,1,0:T(8,128)(2,1)}), bf16[16,32,384]{2,1,0:T(8,128)(2,1)S(1)}, u32[]{:S(2)}, u32[]{:S(2)}) %all-to-all-start.4) | async-done | bytes 393248 | tf_op jit(solution)/shard_map/all_to_all | solution.py:153
  59.4 7.0 %all-to-all-start.1 = ((bf16[16,32,384]{2,1,0:T(8,128)(2,1)}), bf16[16,32,384]{2,1,0:T(8,128)(2,1)S(1)}, u32[]{:S(2)}, u32[]{:S(2)}) async-start(bf16[16,32,384]{2,1,0:T(8,128)(2,1)} %bitcast.1), calls=%async_computation.1 | async-start | bytes 786432 | tf_op jit(solution)/shard_map/all_to_all | solution.py:56
  66.5 2.7 convolution_bitcast_fusion
  69.6 9.1 %all-to-all-done.1 = bf16[16,32,384]{2,1,0:T(8,128)(2,1)S(1)} async-done(((bf16[16,32,384]{2,1,0:T(8,128)(2,1)}), bf16[16,32,384]{2,1,0:T(8,128)(2,1)S(1)}, u32[]{:S(2)}, u32[]{:S(2)}) %all-to-all-start.1) | async-done | bytes 393248 | tf_op jit(solution)/shard_map/all_to_all | solution.py:56
  78.7 2.4 scatter_custom_fusion
  81.1 9.5 %all_to_all.71 = bf16[2,256,384]{2,1,0:T(8,128)(2,1)S(1)} all-to-all(bf16[2,256,384]{2,1,0:T(8,128)(2,1)S(1)} %bitcast.179), channel_id=1, replica_groups=mesh['dp'=16,'seq'=2] {'seq'}, dimensions={0} | all-to-all | bytes 786432 | tf_op jit(solution)/shard_map/all_to_all | solution.py:63
  91.6 3.1 convolution_convert_fusion
  95.2 1.1 pad_maximum_fusion
  96.5 5.2 %add.164 = f32[2048,384]{0,1:T(8,128)} add(f32[2048,384]{0,1:T(8,128)} %convolution_bitcast_fusion, f32[2048,384]{0,1:T(8,128)} %collective-permute-done) | non-fusion elementwise | flops 786432 | bytes 9437184 | tf_op jit(solution)/shard_map/add | solution.py:18
  101.7 0.8 collective-permute-start.1
  104.4 0.9 copy.165
  105.3 0.9 copy.126
  106.2 1.9 select_reduce_fusion
  108.1 0.6 copy-done.5
  108.7 2.5 fusion.1
  111.2 2.7 copy.130
  114.0 2.0 fusion
  116.0 59.3 %collective-permute-done.1 = f32[2048,384]{0,1:T(8,128)} collective-permute-done((f32[2048,384]{0,1:T(8,128)}, f32[2048,384]{0,1:T(8,128)}, u32[]{:S(2)}, u32[]{:S(2)}) %collective-permute-start.1) | collective-permute-done | bytes 3145760 | tf_op jit(solution)/shard_map/ppermute | solution.py:18
  175.3 3.3 add.165
  178.6 1.7 collective-permute-start.2
  180.4 2.5 fusion.27
  182.9 1.6 reshape_reshape.3
  184.5 0.8 copy.143
  185.3 0.8 copy.160
  186.1 1.4 constant_dynamic-update-slice_fusion.11
  187.5 1.4 constant_dynamic-update-slice_fusion.10
  188.9 1.4 constant_dynamic-update-slice_fusion.9
  190.3 1.4 constant_dynamic-update-slice_fusion.8
  191.6 1.4 constant_dynamic-update-slice_fusion.7
  193.0 1.4 constant_dynamic-update-slice_fusion.6
  194.4 1.4 constant_dynamic-update-slice_fusion.5
  195.8 1.4 constant_dynamic-update-slice_fusion.4
  197.1 1.4 constant_dynamic-update-slice_fusion.3
  198.5 1.4 constant_dynamic-update-slice_fusion.2
  199.9 2.8 slice_reduce_fusion.12
  202.7 3.4 slice_reduce_fusion
  206.0 1.9 fusion.29
  208.0 39.6 %collective-permute-done.2 = f32[2048,384]{0,1:T(8,128)} collective-permute-done((f32[2048,384]{0,1:T(8,128)S(1)}, f32[2048,384]{0,1:T(8,128)}, u32[]{:S(2)}, u32[]{:S(2)}) %collective-permute-start.2) | collective-permute-done | bytes 3145760 | tf_op jit(solution)/shard_map/ppermute | solution.py:18
  247.7 4.0 %add.166 = f32[2048,384]{0,1:T(8,128)} add(f32[2048,384]{0,1:T(8,128)S(1)} %add.165, f32[2048,384]{0,1:T(8,128)} %collective-permute-done.2) | non-fusion elementwise | flops 786432 | bytes 9437184 | tf_op jit(solution)/shard_map/add | solution.py:18
  251.7 0.7 collective-permute-start.3
  252.4 0.6 constant_dynamic-update-slice_fusion.1
  253.1 0.7 stack.87
  253.8 0.6 constant_dynamic-update-slice_fusion
  254.5 2.1 copy.156
  256.6 8.1 %gather_fusion = bf16[1536,128]{1,0:T(8,128)(2,1)S(1)} fusion(bf16[512,12,128]{2,0,1:T(8,128)(2,1)S(1)} %copy.156, s32[1536]{0:T(1024)S(1)} %fusion.21), kind=kCustom, calls=%fused_computation | custom fusion | bytes 798720 | tf_op jit(solution)/shard_map/gather | solution.py:110
  265.6 1.5 convolution_add_fusion
  268.0 0.7 select_select_fusion
  268.9 2.5 fusion.6
  271.5 116.8 %collective-permute-done.3 = f32[2048,384]{0,1:T(8,128)} collective-permute-done((f32[2048,384]{0,1:T(8,128)}, f32[2048,384]{0,1:T(8,128)}, u32[]{:S(2)}, u32[]{:S(2)}) %collective-permute-start.3) | collective-permute-done | bytes 3145760 | tf_op jit(solution)/shard_map/ppermute | solution.py:18
  388.3 5.4 %add.167 = f32[2048,384]{0,1:T(8,128)} add(f32[2048,384]{0,1:T(8,128)} %add.166, f32[2048,384]{0,1:T(8,128)} %collective-permute-done.3) | non-fusion elementwise | flops 786432 | bytes 9437184 | tf_op jit(solution)/shard_map/add | solution.py:18
  393.6 3.5 copy.166
  (78 shorter events, 5.9 us)
Async XLA Ops:
  7.2 33.5 %copy-start = (bf16[512,2048]{1,0:T(8,128)(2,1)S(1)}, bf16[512,2048]{1,0:T(8,128)(2,1)}, u32[]{:S(2)}) copy-start(bf16[512,2048]{1,0:T(8,128)(2,1)} %param.8) | copy-start | bytes 6291460
  7.2 84.4 %all-gather.4.cloned.1.call-start = ((), (), s32[]{:S(2)}) async-start(), calls=%async_computation.5 | async-start | bytes 3760128 | tf_op jit(solution)/shard_map/all_gather | solution.py:70
  10.5 13.7 %all-to-all-start = ((s32[16,32,1]{1,2,0:T(1,128)}), s32[16,32,1]{1,2,0:T(1,128)S(1)}, u32[]{:S(2)}, u32[]{:S(2)}) async-start(s32[16,32,1]{1,2,0:T(1,128)} %all_to_all.50), calls=%async_computation | async-start | bytes 16384 | tf_op jit(solution)/shard_map/all_to_all | solution.py:57
  24.2 10.3 %all-to-all-start.3 = ((bf16[256,2,384]{2,0,1:T(8,128)(2,1)}), bf16[256,2,384]{2,0,1:T(8,128)(2,1)S(1)}, u32[]{:S(2)}, u32[]{:S(2)}) async-start(bf16[256,2,384]{2,0,1:T(8,128)(2,1)} %copy.164), calls=%async_computation.3 | async-start | bytes 786432 | tf_op jit(solution)/shard_map/all_to_all | solution.py:146
  37.1 22.3 %all-to-all-start.4 = ((bf16[16,32,384]{2,1,0:T(8,128)(2,1)}), bf16[16,32,384]{2,1,0:T(8,128)(2,1)S(1)}, u32[]{:S(2)}, u32[]{:S(2)}) async-start(bf16[16,32,384]{2,1,0:T(8,128)(2,1)} %bitcast.50), calls=%async_computation.4 | async-start | bytes 786432 | tf_op jit(solution)/shard_map/all_to_all | solution.py:153
  59.4 19.2 %all-to-all-start.1 = ((bf16[16,32,384]{2,1,0:T(8,128)(2,1)}), bf16[16,32,384]{2,1,0:T(8,128)(2,1)S(1)}, u32[]{:S(2)}, u32[]{:S(2)}) async-start(bf16[16,32,384]{2,1,0:T(8,128)(2,1)} %bitcast.1), calls=%async_computation.1 | async-start | bytes 786432 | tf_op jit(solution)/shard_map/all_to_all | solution.py:56
  66.5 188.0 %all-gather.6.cloned.1.call-start = ((), (), s32[]{:S(2)}) async-start(), calls=%async_computation.6 | async-start | bytes 2359296 | tf_op jit(solution)/shard_map/all_gather | solution.py:99
  69.2 22.2 %copy-start.9 = (f32[768]{0:T(1024)S(1)}, f32[768]{0:T(1024)}, u32[]{:S(2)}) copy-start(f32[768]{0:T(1024)} %param.13) | copy-start | bytes 9220
  69.2 27.3 %collective-permute-start = (f32[2048,384]{0,1:T(8,128)}, f32[2048,384]{0,1:T(8,128)}, u32[]{:S(2)}, u32[]{:S(2)}) collective-permute-start(f32[2048,384]{0,1:T(8,128)} %convolution_bitcast_fusion), channel_id=1, source_target_pairs={{0,2},{2,0},{4,6},{6,4},{8,10},{10,8},{12,14},{14,12},{16,18},{18,... | collective-permute-start | bytes 9437192 | tf_op jit(solution)/shard_map/ppermute | solution.py:18
  95.0 6.7 %copy-start.4 = (bf16[256,768]{0,1:T(8,128)(2,1)}, bf16[256,768]{0,1:T(8,128)(2,1)S(1)}, u32[]{:S(2)}) copy-start(bf16[256,768]{0,1:T(8,128)(2,1)S(1)} %copy.128) | copy-start | bytes 1179652
  95.2 11.0 %copy-start.2 = (bf16[256,768]{0,1:T(8,128)(2,1)}, bf16[256,768]{0,1:T(8,128)(2,1)S(1)}, u32[]{:S(2)}) copy-start(bf16[256,768]{0,1:T(8,128)(2,1)S(1)} %copy.127) | copy-start | bytes 1179652
  96.3 172.6 %all-gather.8.cloned.1.call-start = ((), (), s32[]{:S(2)}) async-start(), calls=%async_computation.7 | async-start | bytes 1253376 | tf_op jit(solution)/shard_map/all_gather | solution.py:143
  101.7 73.6 %collective-permute-start.1 = (f32[2048,384]{0,1:T(8,128)}, f32[2048,384]{0,1:T(8,128)}, u32[]{:S(2)}, u32[]{:S(2)}) collective-permute-start(f32[2048,384]{0,1:T(8,128)} %add.164), channel_id=1, source_target_pairs={{0,4},{2,6},{4,0},{6,2},{8,12},{10,14},{12,8},{14,10},{16,20},{18,... | collective-permute-start | bytes 9437192 | tf_op jit(solution)/shard_map/ppermute | solution.py:18
  108.1 0.6 copy-start.5
  178.6 69.0 %collective-permute-start.2 = (f32[2048,384]{0,1:T(8,128)S(1)}, f32[2048,384]{0,1:T(8,128)}, u32[]{:S(2)}, u32[]{:S(2)}) collective-permute-start(f32[2048,384]{0,1:T(8,128)S(1)} %add.165), channel_id=1, source_target_pairs={{0,8},{2,10},{4,12},{6,14},{8,0},{10,2},{12,4},{14,6},{16,24},{18,... | collective-permute-start | bytes 9437192 | tf_op jit(solution)/shard_map/ppermute | solution.py:18
  208.0 44.4 %copy-start.7 = (f32[1,64,1,64]{3,2,1,0:T(1,128)S(1)}, f32[1,64,1,64]{3,2,1,0:T(1,128)}, u32[]{:S(2)}) copy-start(f32[1,64,1,64]{3,2,1,0:T(1,128)} %get-tuple-element.42) | copy-start | bytes 49156
  208.0 45.8 %copy-start.6 = (f32[1,64,1,64]{3,2,1,0:T(1,128)S(1)}, f32[1,64,1,64]{3,2,1,0:T(1,128)}, u32[]{:S(2)}) copy-start(f32[1,64,1,64]{3,2,1,0:T(1,128)} %get-tuple-element.41) | copy-start | bytes 49156
  251.7 136.6 %collective-permute-start.3 = (f32[2048,384]{0,1:T(8,128)}, f32[2048,384]{0,1:T(8,128)}, u32[]{:S(2)}, u32[]{:S(2)}) collective-permute-start(f32[2048,384]{0,1:T(8,128)} %add.166), channel_id=1, source_target_pairs={{0,16},{2,18},{4,20},{6,22},{8,24},{10,26},{12,28},{14,30},{16,0},... | collective-permute-start | bytes 9437192 | tf_op jit(solution)/shard_map/ppermute | solution.py:18
  265.5 3.2 copy-start.3
  267.1 1.7 copy-start.8
  388.3 8.9 %copy-start.1 = (bf16[512,2048]{1,0:T(8,128)(2,1)S(1)}, bf16[512,2048]{1,0:T(8,128)(2,1)}, u32[]{:S(2)}) copy-start(bf16[512,2048]{1,0:T(8,128)(2,1)} %param.8) | copy-start | bytes 6291460
Sparse Core Ops, SparseCore 0:
  10.3 56.5 all-gather.3
  96.4 25.2 all-gather.5
  124.0 41.0 all-gather.7
